TPU v7x, 512 devices: a whole 4x4x16 slice. The times are simulated.
512 devices in a mesh: sweep: 16 (over z_lo, core), dof: 32 (over y, x, z_hi).
Axes of the slice: x: 4, y: 4, z: 16 (z_hi: 2, z_lo: 8; z = z_hi * 8 + z_lo), core: 2. Of those that a mesh axis runs over, the one named last changes fastest.
Arguments:
- mode_shapes: bfloat16 [32, 3, 10240, 256], P('sweep', None, 'dof'), may hold values from -6 to 6
- mass_blocks: float32 [3, 3, 8, 10240], P(None, None, None, 'dof'), may hold values from -0.01171875 to 0.01171875
- block_cols: int32 [8, 10240], P(None, 'dof'), may hold values from 0 to 575, as said below
- send_lists: int32 [32, 2, 128], P('dof'), may hold values from 0 to 319, as said below
Outputs:
- margins: float32 [256, 32, 256], P('dof', 'sweep')
Inputs may be any that keep to these rules, and one draw needn't show every extreme that they name: `block_cols`: slot 0 of node n's block row is the node itself (n modulo 320); other slots point anywhere in the extended list of 576 nodes. `send_lists`: local node indices of the sending partition.
All inputs are finite; a program needn't handle non-finite values.
Results may differ from a plain program's by a relative error of at most 0.0029.
Values may be sent and summed in bfloat16 or wider, within the bound.
A program may use at most 64 MiB of HBM per device.

v0:
```python
import jax
import jax.numpy as jnp
from jax import lax
from jax.sharding import PartitionSpec as P


def passed_along(x, axis, by):
    length = lax.axis_size(axis)
    return lax.ppermute(x, axis, [(i, (i + by) % length) for i in range(length)])


def from_behind(value, axis, steps):
    count = lax.axis_size(axis)
    first, last = (max(0, -steps), min(count, count - steps))
    return lax.ppermute(value, axis, [(source, source + steps) for source in range(first, last)])


def apply_mass(fields, send_lists, block_cols, mass_blocks):
    to_right = jnp.take(fields, send_lists[0, 0], axis=2)
    to_left = jnp.take(fields, send_lists[0, 1], axis=2)
    from_left = passed_along(to_right, "dof", 1)
    from_right = passed_along(to_left, "dof", -1)
    extended = jnp.concatenate([fields, from_left, from_right], axis=2)
    running = jnp.zeros(fields.shape, jnp.float32)
    for column in range(block_cols.shape[0]):
        gathered = jnp.take(extended, block_cols[column], axis=2)
        for component in range(3):
            running = running + mass_blocks[None, :, component, column, :, None] * gathered[
                :, component
            ][:, None].astype(jnp.float32)
    return running.astype(jnp.bfloat16)


def local(mode_shapes, mass_blocks, block_cols, send_lists):
    steps_here = mode_shapes.shape[0]
    is_last = lax.axis_index("sweep") == lax.axis_size("sweep") - 1
    images = apply_mass(mode_shapes, send_lists, block_cols, mass_blocks)
    received = from_behind(images[0], "sweep", -1)
    following = jnp.where(is_last, images[steps_here - 1], received)
    partners = jnp.concatenate([images[1:], following[None]], axis=0)
    row_share = mode_shapes.shape[3] // lax.axis_size("dof")
    partial_terms = jnp.einsum(
        "scnk,scnj->ksj", mode_shapes, partners, preferred_element_type=jnp.float32
    )
    summed = lax.psum(partial_terms, "dof")
    return lax.dynamic_slice_in_dim(summed, lax.axis_index("dof") * row_share, row_share, 0)


def solution(mesh):
    return jax.shard_map(
        local,
        mesh=mesh,
        in_specs=(
            P("sweep", None, "dof", None),
            P(None, None, None, "dof"),
            P(None, "dof"),
            P("dof", None, None),
        ),
        out_specs=P("dof", "sweep", None),
        check_vma=False,
    )
```

profile of v0, /device:TPU:26, one launch (start us, length us, event | category | flops | bytes accessed | tf_op | source)
XLA Modules:
  0.0 790.8 jit_solution(5178973571235893577)
XLA Ops:
  6.5 0.8 compare_and_fusion.8
  7.3 2.8 gather_fusion
  10.2 15.7 %collective-permute-start = (bf16[2,3,128,256]{3,2,1,0:T(8,128)(2,1)S(1)}, bf16[2,3,128,256]{3,2,1,0:T(8,128)(2,1)S(1)}, u32[]{:S(2)}, u32[]{:S(2)}) collective-permute-start(bf16[2,3,128,256]{3,2,1,0:T(8,128)(2,1)S(1)} %select_bitcast_fusion.1), channel_id=1, source_target_pairs={{0,1},{1,2},{2,3},{3,4},{4,5},{5,6},{6,7},{7,8},{8,9},{9,10},{10,1... | collective-permute-start | bytes 1179656 | tf_op jit(solution)/shard_map/ppermute | solution.py:9
  26.0 1.8 gather_fusion.1
  27.9 1.9 collective-permute-start.1
  29.9 1.0 copy_dynamic-update-slice_fusion
  32.1 0.6 compare_and_fusion.2
  37.6 0.6 copy_bitcast_fusion.4
  39.4 0.6 copy_bitcast_fusion.22
  40.0 0.6 copy_bitcast_fusion
  41.2 0.6 pad_clamp_fusion.2
  41.8 0.6 pad_clamp_fusion
  42.8 17.3 %collective-permute-done.1 = bf16[2,3,128,256]{3,2,1,0:T(8,128)(2,1)S(1)} collective-permute-done((bf16[2,3,128,256]{3,2,1,0:T(8,128)(2,1)S(1)}, bf16[2,3,128,256]{3,2,1,0:T(8,128)(2,1)S(1)}, u32[]{:S(2)}, u32[]{:S(2)}) %collective-permute-start.1) | collective-permute-done | bytes 393248 | tf_op jit(solution)/shard_map/ppermute | solution.py:9
  60.6 5.4 gather_fusion.2
  66.0 2.5 fusion.3
  68.6 1.5 fusion.35
  70.1 0.9 copy.11
  71.0 5.1 gather_fusion.3
  76.2 2.5 fusion.4
  78.7 0.7 fusion.32
  79.4 0.9 copy.12
  80.3 0.9 copy.13
  81.2 0.9 copy.14
  82.1 5.1 gather_fusion.4
  87.2 2.5 fusion.5
  89.7 0.7 fusion.29
  90.4 0.9 copy.15
  91.4 0.9 copy.16
  92.2 0.9 copy.17
  93.1 5.4 gather_fusion.5
  98.5 2.5 fusion.6
  101.0 0.7 fusion.26
  101.7 0.9 copy.18
  102.6 0.9 copy.19
  103.5 0.9 copy.20
  104.4 5.1 gather_fusion.6
  109.6 2.5 fusion.7
  112.1 0.7 fusion.23
  112.8 0.9 copy.21
  113.7 0.9 copy.22
  114.6 0.9 copy.23
  115.6 5.1 gather_fusion.7
  120.7 2.5 fusion.8
  123.2 0.7 fusion.20
  123.9 0.9 copy.24
  124.8 0.9 copy.25
  125.7 0.9 copy.26
  126.6 5.4 gather_fusion.8
  132.0 2.5 fusion.9
  134.5 0.7 fusion.17
  135.2 0.9 copy.27
  136.1 1.0 copy.28
  137.1 0.9 copy.29
  138.0 0.9 copy.9
  138.9 5.1 gather_fusion.9
  144.0 2.7 fusion.10
  146.9 0.7 fusion.14
  149.9 6.1 add_convert_fusion
  156.1 1.3 collective-permute-start.2
  157.4 2.5 collective-permute-done.2
  159.9 1.3 convolution_bitcast_fusion
  161.3 620.4 %all-reduce.2.cloned.1.call-done = f32[256,2,256]{0,2,1:T(8,128)} async-done(((f32[256,2,256]{0,2,1:T(8,128)}), f32[256,2,256]{0,2,1:T(8,128)}) %all-reduce.2.cloned.1.call-update) | async-done | bytes 524304 | tf_op jit(solution)/shard_map/psum | solution.py:45
  781.8 1.1 constant_dynamic-slice_fusion
  782.8 0.7 copy.33
  (148 shorter events, 11.3 us)
Async XLA Ops:
  6.5 775.2 %all-reduce.2.cloned.1.call-start = ((), (), s32[]{:S(2)}) async-start(), calls=%async_computation | async-start | bytes 1048576 | tf_op jit(solution)/shard_map/psum | solution.py:45
  7.3 18.7 %copy-start = (bf16[2,3,320,256]{3,2,1,0:T(8,128)(2,1)S(1)}, bf16[2,3,320,256]{3,2,1,0:T(8,128)(2,1)}, u32[]{:S(2)}) copy-start(bf16[2,3,320,256]{3,2,1,0:T(8,128)(2,1)} %param.8) | copy-start | bytes 2949124
  10.2 32.2 %collective-permute-start = (bf16[2,3,128,256]{3,2,1,0:T(8,128)(2,1)S(1)}, bf16[2,3,128,256]{3,2,1,0:T(8,128)(2,1)S(1)}, u32[]{:S(2)}, u32[]{:S(2)}) collective-permute-start(bf16[2,3,128,256]{3,2,1,0:T(8,128)(2,1)S(1)} %select_bitcast_fusion.1), channel_id=1, source_target_pairs={{0,1},{1,2},{2,3},{3,4},{4,5},{5,6},{6,7},{7,8},{8,9},{9,10},{10,1... | collective-permute-start | bytes 1179656 | tf_op jit(solution)/shard_map/ppermute | solution.py:9
  27.8 3.1 copy-start.38
  27.8 4.9 copy-start.15
  27.9 32.2 %collective-permute-start.1 = (bf16[2,3,128,256]{3,2,1,0:T(8,128)(2,1)S(1)}, bf16[2,3,128,256]{3,2,1,0:T(8,128)(2,1)S(1)}, u32[]{:S(2)}, u32[]{:S(2)}) collective-permute-start(bf16[2,3,128,256]{3,2,1,0:T(8,128)(2,1)S(1)} %select_bitcast_fusion), channel_id=1, source_target_pairs={{0,31},{1,0},{2,1},{3,2},{4,3},{5,4},{6,5},{7,6},{8,7},{9,8},{10,9... | collective-permute-start | bytes 1179656 | tf_op jit(solution)/shard_map/ppermute | solution.py:9
  42.4 23.6 %copy-start.53 = (pred[320]{0:T(512)(128)(4,1)S(1)}, pred[320]{0:T(512)(128)(4,1)}, u32[]{:S(2)}) copy-start(pred[320]{0:T(512)(128)(4,1)} %get-tuple-element.86) | copy-start | bytes 964
  70.1 1.0 copy-start.43
  70.1 6.0 copy-start.52
  79.4 2.7 copy-start.41
  81.2 6.0 copy-start.51
  90.4 2.7 copy-start.40
  92.2 6.3 copy-start.50
  101.7 2.7 copy-start.45
  103.5 6.0 copy-start.49
  112.8 2.8 copy-start.44
  114.6 6.1 copy-start.47
  123.9 2.7 copy-start.42
  125.7 6.3 copy-start.48
  135.2 2.8 copy-start.14
  136.1 2.8 copy-start.39
  138.0 6.0 copy-start.46
  144.0 3.9 copy-start.11
  144.0 3.9 copy-start.12
  144.0 3.9 copy-start.13
  146.7 1.2 copy-start.7
  146.7 1.3 copy-start.8
  146.7 1.5 copy-start.9
  146.7 1.7 copy-start.10
  146.8 1.6 copy-start.24
  146.8 1.6 copy-start.25
  146.8 1.6 copy-start.26
  146.8 1.6 copy-start.27
  146.8 1.6 copy-start.28
  146.8 1.6 copy-start.29
  146.8 1.6 copy-start.30
  146.8 1.6 copy-start.31
  146.8 1.6 copy-start.32
  146.8 1.6 copy-start.33
  146.9 1.6 copy-start.34
  146.9 1.6 copy-start.35
  146.9 1.6 copy-start.36
  146.9 1.6 copy-start.37
  147.6 1.3 copy-start.1
  147.6 1.5 copy-start.2
  147.6 1.7 copy-start.3
  147.6 1.9 copy-start.4
  147.6 2.1 copy-start.5
  147.6 2.2 copy-start.6
  147.6 2.2 copy-start.16
  147.7 2.2 copy-start.17
  147.7 2.2 copy-start.18
  147.7 2.2 copy-start.19
  147.7 2.2 copy-start.20
  147.7 2.2 copy-start.21
  147.7 2.2 copy-start.22
  147.7 2.2 copy-start.23
  156.1 3.8 collective-permute-start.2
Sparse Core Ops, SparseCore 0:
  161.4 620.2 all-reduce.1
where the time goes:
time: 796 us; the launch traced here: 791 us
  waiting for transfers between devices  640 us (80%)
  local copies, waits for them, and re-layouts  77.2 us (10%)
  other arithmetic  38.5 us (5%)
  starting transfers between devices  18.9 us (2%)
  between operations  14.7 us (2%)
    psum x1, waiting for transfers between devices, local(): summed = lax.psum(partial_terms, 'dof')  620 us
    gather x8, local copies, waits for them, and re-layouts, apply_mass(): gathered = jnp.take(extended, block_cols[column], axis=2)  41.9 us
    select_n x16, other arithmetic, apply_mass(): gathered = jnp.take(extended, block_cols[column], axis=2)  20.4 us
    mul x24, local copies, waits for them, and re-layouts, apply_mass(): mass_blocks[None, :, component, column, :, None]  18.2 us
    ppermute x2, starting transfers between devices, passed_along(): lax.ppermute(x, axis, [(i, (i + by) % length) for i in range(length)])  17.6 us
    ppermute x2, waiting for transfers between devices, passed_along(): lax.ppermute(x, axis, [(i, (i + by) % length) for i in range(length)])  17.3 us
  transfers between devices with their start and end apart: 4, of which 3 were waited for; matrix products, arithmetic and copies ran while one was open for 2% of the time, Pallas kernels for 0%

commit v1 on v0

v1 whole, which is shorter than its diff:
```python
import jax
import jax.numpy as jnp
from jax import lax
from jax.experimental import pallas as pl
from jax.experimental.pallas import tpu as pltpu
from jax.sharding import PartitionSpec as P

MESH = pl.DeviceIdType.MESH
F32, BF16 = jnp.float32, jnp.bfloat16
HALVES = 2


def dot(a, b):
    return jnp.dot(a, b, preferred_element_type=F32)


def dot_t(a, b):
    return lax.dot_general(a, b, (((0,), (0,)), ((), ())), preferred_element_type=F32)


def margins_kernel(n_sweep, n_dof, modes, mass, cols, lists, out, fq, fr, cb, pk_own, pk_q, pk_r, cols3, mt_hi, mt_lo,
                   mq_hi, mq_lo, mr_hi, mr_lo, ya_own, ya_halo, yb, gt_q, gt_r, cs_q, cs_r, part, acc_bt, rsb, tot, last,
                   z_ss, z_rs, x_ss, x_rs, m_ss, m_rs, r_ss, r_rs):
    nodes, halo, width = cols.shape[1], lists.shape[2], modes.shape[2]
    rows = 3 * nodes
    planes = n_dof // 2
    z_lo_n = n_sweep // 2
    half = width // HALVES
    w, p = lax.axis_index("sweep"), lax.axis_index("dof")
    core, z_lo = lax.rem(w, 2), w // 2
    k, z_hi = p // 2, lax.rem(p, 2)
    far = {"dof": 2 * k + (1 - z_hi)}

    def plane(kk):
        return {"dof": 2 * lax.rem(kk + planes, planes) + z_hi}

    def z_step(by):
        moved = z_lo + by
        wrapped = jnp.logical_or(moved < 0, moved >= z_lo_n)
        lo = lax.rem(moved + z_lo_n, z_lo_n)
        hi = jnp.where(wrapped, 1 - z_hi, z_hi)
        return {"sweep": lo * 2 + core, "dof": 2 * k + hi}

    def sweep_step(by):
        return {"sweep": lax.rem(w + by + n_sweep, n_sweep)}

    towards = jnp.where(z_lo < z_lo_n // 2, 1, -1)
    depth = jnp.where(z_lo < z_lo_n // 2, z_lo, z_lo_n - 1 - z_lo)
    is_first, is_last = w == 0, w == n_sweep - 1

    barrier = pltpu.get_barrier_semaphore()
    greeted = [far, sweep_step(1), sweep_step(-1), z_step(1), z_step(-1)]
    greeted += [plane(k + t) for t in range(1, planes)]
    for device in greeted:
        pl.semaphore_signal(barrier, inc=1, device_id=device, device_id_type=MESH)
    pl.semaphore_wait(barrier, len(greeted))

    def remote(src, dst, send, recv, device):
        return pltpu.make_async_remote_copy(src_ref=src, dst_ref=dst, send_sem=send, recv_sem=recv, device_id=device,
                                            device_id_type=MESH)

    chunks = [(c, h) for h in range(HALVES) for c in range(3)]

    def piece(ref, c, h):
        return ref.at[pl.ds(c * nodes, nodes), pl.ds(h * half, half)]

    x_next = plane(k + 1 - 2 * z_hi)
    z_copies = [remote(piece(modes.at[1], c, h), piece(fq, c, h), z_ss.at[i], z_rs.at[i], far) for i, (c, h) in enumerate(chunks)]
    x_copies = [remote(piece(fq, c, h), piece(fr, c, h), x_ss.at[i], x_rs.at[i], x_next) for i, (c, h) in enumerate(chunks)]
    for copy in z_copies:
        copy.start()
    c_copy = remote(modes.at[0], cb, m_ss.at[0], m_rs.at[0], sweep_step(-1))

    @pl.when(w > 0)
    def _():
        c_copy.start()

    for d in range(3):
        pk_own[d] = jnp.concatenate([mass[c, d] for c in range(3)], axis=1)
    pk_own[3, :, 0:nodes] = cols[...].astype(F32)
    pk_own[3, 0:2, 384:384 + halo] = lists[0].astype(F32)

    mine = pl.ds(2 * core, 2)
    own_copy = remote(pk_own.at[mine], pk_q.at[mine], m_ss.at[1], m_rs.at[1], z_step(-towards))
    chain_copy = remote(pk_q.at[mine], pk_q.at[mine], m_ss.at[2], m_rs.at[1], z_step(towards))
    core_copy = remote(pk_q.at[mine], pk_q.at[mine], m_ss.at[3], m_rs.at[2], {"sweep": z_lo * 2 + 1 - core})
    pack_copy = remote(pk_q, pk_r, m_ss.at[4], m_rs.at[3], x_next)

    @pl.when(depth == 0)
    def _():
        own_copy.start()

    def build(pk, offset, count, hi, lo):
        one = pk[3, :, 0:nodes]
        cols3[...] = jnp.concatenate([one, one, one], axis=1)

        def body(g, carry):
            r = pl.multiple_of(g * 16, 16)
            for lane, lanes in ((0, 512), (512, rows - 512)):
                ids = (lax.broadcasted_iota(jnp.int32, (16, lanes), 0) + (r + offset)).astype(F32)
                sums = [jnp.zeros((16, lanes), F32) for _ in range(3)]
                for b in range(8):
                    hit = ids == cols3[b:b + 1, lane:lane + lanes]
                    for d in range(3):
                        sums[d] = sums[d] + jnp.where(hit, pk[d, b:b + 1, lane:lane + lanes], 0.0)
                for d in range(3):
                    top = sums[d].astype(BF16)
                    hi[d, pl.ds(r, 16), lane:lane + lanes] = top
                    lo[d, pl.ds(r, 16), lane:lane + lanes] = (sums[d] - top.astype(F32)).astype(BF16)
            return carry

        lax.fori_loop(0, count // 16, body, 0)

    def one_hot(row):
        ids = lax.broadcasted_iota(jnp.int32, (nodes, halo), 0).astype(F32)
        return jnp.where(ids == row, 1.0, 0.0).astype(BF16)

    build(pk_own, 0, nodes + 2 * halo, mt_hi, mt_lo)

    own_copy.wait_recv()

    @pl.when(depth < z_lo_n // 2 - 1)
    def _():
        chain_copy.start()

    core_copy.start()

    for d in range(3):
        first = dot(mt_hi[d], modes[0]) + dot(mt_lo[d], modes[0])
        ya_own[pl.ds(d * nodes, nodes), :] = first[0:nodes].astype(BF16)
        ya_halo[d] = first[nodes:].astype(BF16)
    part[0] = dot_t(ya_own[...], modes[1])

    core_copy.wait_recv()
    pack_copy.start()

    for d in range(3):
        second = dot(mt_hi[d, 0:nodes], modes[1]) + dot(mt_lo[d, 0:nodes], modes[1])
        yb[pl.ds(d * nodes, nodes), :] = second.astype(BF16)

    @pl.when(jnp.logical_not(is_last))
    def _():
        c_copy.wait_recv()

    @pl.when(is_last)
    def _():
        cb[...] = modes[1]

    acc_bt[...] = dot_t(cb[...], yb[...])

    def side(pk, seg_here, row_there, seg_there, row_here, hi, lo, gt, cs):
        there = one_hot(jnp.where(row_there == 0, pk[3, 0:1, 384:384 + halo], pk[3, 1:2, 384:384 + halo]))
        here = one_hot(jnp.where(row_here == 0, lists[0, 0:1, :], lists[0, 1:2, :]).astype(F32))
        build(pk, nodes + halo * seg_there, halo, hi, lo)
        for d in range(3):
            gt[pl.ds(d * nodes, nodes), :] = dot(there, ya_halo[d, pl.ds(pl.multiple_of(halo * seg_here, halo), halo), :]).astype(BF16)
            cs[pl.ds(d * halo, halo), :] = dot_t(here, cb[pl.ds(d * nodes, nodes), :]).astype(BF16)

    def use(field, hi, lo, gt, cs, h):
        lanes = slice(h * half, (h + 1) * half)
        block = field[:, lanes]
        y = (dot(hi[...].reshape(3 * halo, rows), block) + dot(lo[...].reshape(3 * halo, rows), block)).astype(BF16)
        acc_bt[:, lanes] += dot_t(cs[...], y)
        part[0, :, lanes] += dot_t(gt[...], block)

    side(pk_q, 1 - z_hi, 1 - z_hi, z_hi, z_hi, mq_hi, mq_lo, gt_q, cs_q)
    z_copies[0].wait_recv()
    x_copies[0].start()
    pack_copy.wait_recv()
    side(pk_r, z_hi, z_hi, 1 - z_hi, 1 - z_hi, mr_hi, mr_lo, gt_r, cs_r)

    for h in range(HALVES):
        for i, (c, hh) in enumerate(chunks):
            if hh == h and i > 0:
                z_copies[i].wait_recv()
                x_copies[i].start()
        use(fq, mq_hi, mq_lo, gt_q, cs_q, h)
        for i, (c, hh) in enumerate(chunks):
            if hh == h:
                x_copies[i].wait_recv()
        use(fr, mr_hi, mr_lo, gt_r, cs_r, h)

    part[1] = acc_bt[...].T

    share = width // n_dof
    pair = 2 * share
    sends = []
    for t in range(1, planes):
        there = lax.rem(k + t, planes)
        sends.append(remote(part.at[:, pl.ds(pl.multiple_of(there * pair, pair), pair), :], rsb.at[t - 1], r_ss.at[t - 1],
                            r_rs.at[t - 1], plane(k + t)))
    for copy in sends:
        copy.start()
    total = part[:, pl.ds(pl.multiple_of(k * pair, pair), pair), :]
    for t, copy in enumerate(sends):
        copy.wait_recv()
        total = total + rsb[t]
    tot[:, 0] = total[:, 0:share]
    tot[:, 1] = total[:, share:]
    last_copy = remote(tot.at[:, 1 - z_hi], last, m_ss.at[5], m_rs.at[4], far)
    last_copy.start()

    for copy in z_copies + x_copies + sends:
        copy.wait_send()

    @pl.when(w > 0)
    def _():
        c_copy.wait_send()

    @pl.when(depth == 0)
    def _():
        own_copy.wait_send()

    @pl.when(depth < z_lo_n // 2 - 1)
    def _():
        chain_copy.wait_send()

    core_copy.wait_send()
    pack_copy.wait_send()
    last_copy.wait()
    for s in range(2):
        out[:, s, :] = tot[s, pl.ds(z_hi, 1)][0] + last[s]


def solution(mesh):
    n_sweep, n_dof = mesh.shape["sweep"], mesh.shape["dof"]

    def local(mode_shapes, mass_blocks, block_cols, send_lists):
        _, _, nodes, width = mode_shapes.shape
        halo = send_lists.shape[2]
        rows, planes, share = 3 * nodes, n_dof // 2, width // n_dof
        ext = nodes + 2 * halo
        vmem = pltpu.VMEM
        dma = pltpu.SemaphoreType.DMA
        return pl.pallas_call(
            lambda *refs: margins_kernel(n_sweep, n_dof, *refs),
            out_shape=jax.ShapeDtypeStruct((share, 2, width), F32),
            in_specs=[pl.BlockSpec(memory_space=pltpu.VMEM)] * 4,
            out_specs=pl.BlockSpec(memory_space=pltpu.VMEM),
            scratch_shapes=[
                vmem((rows, width), BF16), vmem((rows, width), BF16), vmem((rows, width), BF16),
                vmem((4, 8, rows), F32), vmem((4, 8, rows), F32), vmem((4, 8, rows), F32), vmem((8, rows), F32),
                vmem((3, ext, rows), BF16), vmem((3, ext, rows), BF16),
                vmem((3, halo, rows), BF16), vmem((3, halo, rows), BF16),
                vmem((3, halo, rows), BF16), vmem((3, halo, rows), BF16),
                vmem((rows, width), BF16), vmem((3, 2 * halo, width), BF16), vmem((rows, width), BF16),
                vmem((rows, width), BF16), vmem((rows, width), BF16),
                vmem((3 * halo, width), BF16), vmem((3 * halo, width), BF16),
                vmem((2, width, width), F32), vmem((width, width), F32),
                vmem((planes - 1, 2, 2 * share, width), F32),
                vmem((2, 2, share, width), F32), vmem((2, share, width), F32),
                dma((6,)), dma((6,)), dma((6,)), dma((6,)), dma((6,)), dma((5,)), dma((planes - 1,)), dma((planes - 1,)),
            ],
            compiler_params=pltpu.CompilerParams(collective_id=0, has_side_effects=True, vmem_limit_bytes=40 * 2**20),
        )(mode_shapes.reshape(2, rows, width), mass_blocks, block_cols, send_lists)

    return jax.shard_map(
        local,
        mesh=mesh,
        in_specs=(
            P("sweep", None, "dof", None),
            P(None, None, None, "dof"),
            P(None, "dof"),
            P("dof", None, None),
        ),
        out_specs=P("dof", "sweep", None),
        check_vma=False,
    )
```

time: 796 us -> 112 us (0.14)
  the two profiles are of different devices: /device:TPU:26 before, /device:TPU:102 now
where the time goes in v1:
time: 112 us
  Pallas kernels  108 us (96%)
  local copies, waits for them, and re-layouts  4.09 us (4%)
    pallas_call x1, Pallas kernels, local(): pl.pallas_call(lambda *refs: margins_kernel(n_sweep, n_dof, *refs), out_s...  108 us
    unnamed x9, local copies, waits for them, and re-layouts  4.09 us

profile of v1, /device:TPU:102, one launch (start us, length us, event | category | flops | bytes accessed | tf_op | source)
XLA Modules:
  0.0 112.1 jit_solution(1253621607545150847)
XLA Ops:
  0.0 0.0 copy-start.3
  0.0 0.7 copy-done.3
  0.7 0.0 copy-start
  0.7 1.2 %copy-done = bf16[2,3,320,256]{3,2,1,0:T(8,128)(2,1)S(1)} copy-done((bf16[2,3,320,256]{3,2,1,0:T(8,128)(2,1)S(1)}, bf16[2,3,320,256]{3,2,1,0:T(8,128)(2,1)}, u32[]{:S(2)}) %copy-start) | copy-done | bytes 983064
  1.9 0.0 copy-start.1
  1.9 0.9 copy-done.1
  2.8 0.0 copy-start.2
  2.8 0.7 copy-done.2
  3.5 108.0 %shard_map.46 = f32[8,2,256]{2,1,0:T(2,128)S(1)} custom-call(bf16[2,960,256]{2,1,0:T(8,128)(2,1)S(1)} %bitcast.1, f32[3,3,8,320]{3,2,1,0:T(8,128)S(1)} %copy-done.1, s32[8,320]{1,0:T(8,128)S(1)} %copy-done.2, s32[1,2,128]{2,1,0:T(2,128)S(1)} %copy-done.3), custom_call_target="tpu_custom_call" | custom-call | tf_op jit(solution)/shard_map/pallas_call | solution.py:235
  111.5 0.6 copy.6
Async XLA Ops:
  0.0 0.7 copy-start.3
  0.7 1.2 %copy-start = (bf16[2,3,320,256]{3,2,1,0:T(8,128)(2,1)S(1)}, bf16[2,3,320,256]{3,2,1,0:T(8,128)(2,1)}, u32[]{:S(2)}) copy-start(bf16[2,3,320,256]{3,2,1,0:T(8,128)(2,1)} %param.4) | copy-start | bytes 2949124
  1.9 0.9 copy-start.1
  2.8 0.7 copy-start.2

commit v2 on v1

v2 whole, which is shorter than its diff:
```python
import jax
import jax.numpy as jnp
from jax import lax
from jax.experimental import pallas as pl
from jax.experimental.pallas import tpu as pltpu
from jax.sharding import PartitionSpec as P

MESH = pl.DeviceIdType.MESH
F32, BF16 = jnp.float32, jnp.bfloat16
HALVES = 2
GROUP = 2
PARTS = 6
WINDOW = 4
C_PARTS = 6
C_FROM = 0
CUT = 8
PACK = 1024
LISTS = 384


def dot(a, b):
    return jnp.dot(a, b, preferred_element_type=F32)


def dot_t(a, b):
    return lax.dot_general(a, b, (((0,), (0,)), ((), ())), preferred_element_type=F32)


def margins_kernel(n_sweep, n_dof, modes_in, mass_in, cols_in, lists_in, out, modes, mass, cols, lists, fq, fr, cb, mass_own, cols_own, pk_own, pk_q, pk_r, cols_q, cols_r,
                   mt_hi, mt_lo, mq_hi, mq_lo, mr_hi, mr_lo, ya_own, ya_halo, yb, g_q, g_r, cs_q, cs_r, part, acc_bt, rsb, tot,
                   last, z_ss, z_rs, x_ss, x_rs, c_ss, c_rs, m_ss, m_rs, e_ss, e_rs, a_ss, a_rs, b_ss, b_rs, in_s):
    nodes, halo, width = cols.shape[1], lists.shape[2], modes.shape[2]
    rows = 3 * nodes
    planes = n_dof // 2
    half = width // HALVES
    w, p = lax.axis_index("sweep"), lax.axis_index("dof")
    k, z_hi = p // 2, lax.rem(p, 2)
    far = {"dof": 2 * k + (1 - z_hi)}
    seat = lax.rem(w, GROUP)

    def plane(kk):
        return {"dof": 2 * lax.rem(kk + planes, planes) + z_hi}

    def sweep_step(by):
        return {"sweep": lax.rem(w + by + n_sweep, n_sweep)}

    def groupmate(t):
        return {"sweep": w - seat + lax.rem(seat + t, GROUP)}

    is_last = w == n_sweep - 1

    barrier = pltpu.get_barrier_semaphore()
    greeted = [far, sweep_step(1), sweep_step(-1)]
    greeted += [groupmate(t) for t in range(1, GROUP)]
    greeted += [plane(k + t) for t in range(1, planes)]
    for device in greeted:
        pl.semaphore_signal(barrier, inc=1, device_id=device, device_id_type=MESH)

    loads = [pltpu.make_async_copy(src, dst, in_s.at[i])
             for i, (src, dst) in enumerate(((mass_in, mass), (cols_in, cols), (lists_in, lists), (modes_in, modes)))]
    for load in loads:
        load.start()
    for load in loads[0:3]:
        load.wait()

    def wide(parts):
        filled = sum(part.shape[1] for part in parts)
        return jnp.concatenate(parts + [jnp.zeros((parts[0].shape[0], PACK - filled), F32)], axis=1)

    columns = cols[...].astype(F32)
    own_lists = lists[0].astype(F32)
    cols_own[...] = jnp.concatenate([columns] * 3, axis=1)
    for d in range(3):
        block = [mass[c, d] for c in range(3)]
        mass_own[d] = jnp.concatenate(block, axis=1)
        pk_own[d] = wide(block)
    pk_own[0, 0:1, :] = wide([columns[b:b + 1] for b in (1, 2, 3)])
    pk_own[1, 0:1, :] = wide([columns[b:b + 1] for b in (4, 5, 6)])
    pk_own[2, 0:1, :] = wide([columns[7:8], jnp.zeros((1, LISTS - nodes), F32), own_lists[0:1], own_lists[1:2]])

    pl.semaphore_wait(barrier, len(greeted))

    def remote(src, dst, send, recv, device):
        return pltpu.make_async_remote_copy(src_ref=src, dst_ref=dst, send_sem=send, recv_sem=recv, device_id=device,
                                            device_id_type=MESH)

    chunks = [(c, h) for h in range(HALVES) for c in range(PARTS)]

    def piece(ref, c, h):
        return ref.at[pl.ds(c * (rows // PARTS), rows // PARTS), pl.ds(h * half, half)]

    def strip(ref, c):
        return ref.at[pl.ds(c * (rows // C_PARTS), rows // C_PARTS)]

    x_next = plane(k + 1 - 2 * z_hi)
    mine = pl.ds(pl.multiple_of(seat * (PACK // GROUP), PACK // GROUP), PACK // GROUP)
    z_copies = [remote(piece(modes_in.at[1], c, h), piece(fq, c, h), z_ss.at[i], z_rs.at[i], far) for i, (c, h) in enumerate(chunks)]
    x_copies = [remote(piece(fq, c, h), piece(fr, c, h), x_ss.at[i], x_rs.at[i], x_next) for i, (c, h) in enumerate(chunks)]
    c_copies = [remote(strip(modes_in.at[0], i), strip(cb, i), c_ss.at[i], c_rs.at[i], sweep_step(-1)) for i in range(C_PARTS)]
    own_copy = remote(pk_own.at[:, :, mine], pk_q.at[:, :, mine], m_ss.at[1], m_rs.at[1], far)
    e_copies = [remote(pk_q.at[:, :, mine], pk_q.at[:, :, mine], e_ss.at[t - 1], e_rs.at[t - 1], groupmate(t)) for t in range(1, GROUP)]
    pack_copy = remote(pk_q, pk_r, m_ss.at[2], m_rs.at[2], x_next)

    def pump(i):
        z_copies[i].wait_recv()
        x_copies[i].start()
        if i + WINDOW < len(chunks):
            z_copies[i + WINDOW].start()
        if C_FROM <= i < C_FROM + C_PARTS:
            @pl.when(w > 0)
            def _():
                c_copies[i - C_FROM].start()

    own_copy.start()

    @pl.when(w // 2 < CUT)
    def _():
        for i in range(WINDOW):
            z_copies[i].start()

    def build(masses, columns, slots, offset, begin, count, hi, lo):
        def body(g, carry):
            r = pl.multiple_of(g * 16, 16)
            for lane, lanes in ((0, 512), (512, rows - 512)):
                ids = (lax.broadcasted_iota(jnp.int32, (16, lanes), 0) + (r + offset)).astype(F32)
                sums = [jnp.zeros((16, lanes), F32) for _ in range(3)]
                for b in slots:
                    hit = ids == columns[b:b + 1, lane:lane + lanes]
                    for d in range(3):
                        sums[d] = sums[d] + jnp.where(hit, masses[d, b:b + 1, lane:lane + lanes], 0.0)
                for d in range(3):
                    top = sums[d].astype(BF16)
                    hi[d, pl.ds(r, 16), lane:lane + lanes] = top
                    lo[d, pl.ds(r, 16), lane:lane + lanes] = (sums[d] - top.astype(F32)).astype(BF16)
            return carry

        lax.fori_loop(begin // 16, count // 16, body, 0)

    def one_hot(row):
        ids = lax.broadcasted_iota(jnp.int32, (nodes, halo), 0).astype(F32)
        return jnp.where(ids == row, 1.0, 0.0).astype(BF16)

    def side_rows(pk, columns, seg_here, row_there, seg_there, hi, lo, g):
        for b in range(1, 8):
            at = (b - 1) % 3 * nodes
            columns[b:b + 1, :] = jnp.concatenate([pk[(b - 1) // 3, 0:1, at:at + nodes]] * 3, axis=1)
        there = one_hot(jnp.where(row_there == 0, pk[2, 0:1, LISTS:LISTS + halo], pk[2, 0:1, LISTS + halo:LISTS + 2 * halo]))
        build(pk, columns, range(1, 8), nodes + halo * seg_there, 0, halo, hi, lo)
        spread = [dot(there, ya_halo[d, pl.ds(pl.multiple_of(halo * seg_here, halo), halo), :]).T for d in range(3)]
        g[...] = jnp.concatenate(spread, axis=1).astype(BF16)

    def side_partner(row_here, cs):
        here = one_hot(jnp.where(row_here == 0, lists[0, 0:1, :], lists[0, 1:2, :]).astype(F32))
        for d in range(3):
            cs[:, d * halo:(d + 1) * halo] = dot_t(cb[pl.ds(d * nodes, nodes), :], here).astype(BF16)

    def use_first(field, g, h):
        lanes = slice(h * half, (h + 1) * half)
        part[0, :, lanes] += dot(g[...], field[:, lanes])

    def use_second(field, hi, lo, cs, h):
        lanes = slice(h * half, (h + 1) * half)
        block = field[:, lanes]
        y = (dot(hi[...].reshape(3 * halo, rows), block) + dot(lo[...].reshape(3 * halo, rows), block)).astype(BF16)
        acc_bt[:, lanes] += dot(cs[...], y)

    ext = nodes + 2 * halo
    build(mass_own, cols_own, range(8), 0, 0, ext // 2, mt_hi, mt_lo)
    own_copy.wait_recv()
    for copy in e_copies:
        copy.start()
    build(mass_own, cols_own, range(8), 0, ext // 2, ext, mt_hi, mt_lo)

    @pl.when(w // 2 >= CUT)
    def _():
        for i in range(WINDOW):
            z_copies[i].start()

    for copy in e_copies:
        copy.wait_recv()
    pack_copy.start()
    loads[3].wait()

    for d in range(3):
        pump(d)
        first = dot(mt_hi[d], modes[0]) + dot(mt_lo[d], modes[0])
        ya_own[pl.ds(d * nodes, nodes), :] = first[0:nodes].astype(BF16)
        ya_halo[d] = first[nodes:].astype(BF16)
    pump(3)
    part[0] = dot_t(ya_own[...], modes[1])
    for d in range(3):
        second = dot(mt_hi[d, 0:nodes], modes[1]) + dot(mt_lo[d, 0:nodes], modes[1])
        yb[pl.ds(d * nodes, nodes), :] = second.astype(BF16)
    pump(4)
    side_rows(pk_q, cols_q, 1 - z_hi, 1 - z_hi, z_hi, mq_hi, mq_lo, g_q)
    pump(5)
    pack_copy.wait_recv()
    side_rows(pk_r, cols_r, z_hi, z_hi, 1 - z_hi, mr_hi, mr_lo, g_r)
    pump(6)
    use_first(fq, g_q, 0)
    pump(7)

    @pl.when(jnp.logical_not(is_last))
    def _():
        for copy in c_copies:
            copy.wait_recv()

    @pl.when(is_last)
    def _():
        cb[...] = modes[1]

    acc_bt[...] = dot_t(cb[...], yb[...])
    side_partner(z_hi, cs_q)
    side_partner(1 - z_hi, cs_r)
    use_second(fq, mq_hi, mq_lo, cs_q, 0)
    pump(8)

    share = width // n_dof
    pair = 2 * share
    a_copies, b_copies = [], []
    for h in range(HALVES):
        for t in range(1, planes):
            there = pl.ds(pl.multiple_of(lax.rem(k + t, planes) * pair, pair), pair)
            lanes = pl.ds(h * half, half)
            a_copies.append(remote(part.at[0, there, lanes], rsb.at[t - 1, 0, :, lanes], a_ss.at[h, t - 1], a_rs.at[h, t - 1],
                                   plane(k + t)))
            if h == 0:
                b_copies.append(remote(part.at[1, there], rsb.at[t - 1, 1], b_ss.at[t - 1], b_rs.at[t - 1], plane(k + t)))

    for h in range(HALVES):
        lanes = slice(h * half, (h + 1) * half)
        if h > 0:
            for i in range(9, h * PARTS + PARTS):
                pump(i)
            use_first(fq, g_q, h)
            use_second(fq, mq_hi, mq_lo, cs_q, h)
        for i in range(h * PARTS, h * PARTS + PARTS):
            x_copies[i].wait_recv()
        use_first(fr, g_r, h)
        for t in range(1, planes):
            a_copies[h * (planes - 1) + t - 1].start()
        use_second(fr, mr_hi, mr_lo, cs_r, h)
        part[1, lanes, :] = acc_bt[:, lanes].T
        for t in range(1, planes):
            @pl.when(lax.rem(k + t, planes) // (planes // HALVES) == h)
            def _():
                b_copies[t - 1].start()

    total = part[:, pl.ds(pl.multiple_of(k * pair, pair), pair), :]
    for t in range(1, planes):
        for h in range(HALVES):
            a_copies[h * (planes - 1) + t - 1].wait_recv()
        b_copies[t - 1].wait_recv()
        total = total + rsb[t - 1]
    tot[:, 0] = total[:, 0:share]
    tot[:, 1] = total[:, share:]
    last_copy = remote(tot.at[:, 1 - z_hi], last, m_ss.at[3], m_rs.at[3], far)
    last_copy.start()

    for copy in z_copies + x_copies + a_copies + b_copies + e_copies:
        copy.wait_send()

    @pl.when(w > 0)
    def _():
        for copy in c_copies:
            copy.wait_send()

    own_copy.wait_send()
    pack_copy.wait_send()
    last_copy.wait()
    for s in range(2):
        out[:, s, :] = tot[s, pl.ds(z_hi, 1)][0] + last[s]


def solution(mesh):
    n_sweep, n_dof = mesh.shape["sweep"], mesh.shape["dof"]

    def local(mode_shapes, mass_blocks, block_cols, send_lists):
        _, _, nodes, width = mode_shapes.shape
        halo = send_lists.shape[2]
        rows, planes, share = 3 * nodes, n_dof // 2, width // n_dof
        ext = nodes + 2 * halo
        vmem = pltpu.VMEM
        dma = pltpu.SemaphoreType.DMA
        return pl.pallas_call(
            lambda *refs: margins_kernel(n_sweep, n_dof, *refs),
            out_shape=jax.ShapeDtypeStruct((share, 2, width), F32),
            in_specs=[pl.BlockSpec(memory_space=pltpu.HBM)] * 4,
            out_specs=pl.BlockSpec(memory_space=pltpu.VMEM),
            scratch_shapes=[
                vmem((2, rows, width), BF16), vmem(mass_blocks.shape, F32), vmem(block_cols.shape, jnp.int32), vmem(send_lists.shape, jnp.int32),
                vmem((rows, width), BF16), vmem((rows, width), BF16), vmem((rows, width), BF16),
                vmem((3, 8, rows), F32), vmem((8, rows), F32),
                vmem((3, 8, PACK), F32), vmem((3, 8, PACK), F32), vmem((3, 8, PACK), F32), vmem((8, rows), F32), vmem((8, rows), F32),
                vmem((3, ext, rows), BF16), vmem((3, ext, rows), BF16),
                vmem((3, halo, rows), BF16), vmem((3, halo, rows), BF16),
                vmem((3, halo, rows), BF16), vmem((3, halo, rows), BF16),
                vmem((rows, width), BF16), vmem((3, 2 * halo, width), BF16), vmem((rows, width), BF16),
                vmem((width, rows), BF16), vmem((width, rows), BF16),
                vmem((width, 3 * halo), BF16), vmem((width, 3 * halo), BF16),
                vmem((2, width, width), F32), vmem((width, width), F32),
                vmem((planes - 1, 2, 2 * share, width), F32),
                vmem((2, 2, share, width), F32), vmem((2, share, width), F32),
                dma((HALVES * PARTS,)), dma((HALVES * PARTS,)), dma((HALVES * PARTS,)), dma((HALVES * PARTS,)),
                dma((C_PARTS,)), dma((C_PARTS,)), dma((4,)), dma((4,)), dma((GROUP - 1,)), dma((GROUP - 1,)),
                dma((HALVES, planes - 1)), dma((HALVES, planes - 1)), dma((planes - 1,)), dma((planes - 1,)), dma((4,)),
            ],
            compiler_params=pltpu.CompilerParams(collective_id=0, has_side_effects=True, vmem_limit_bytes=40 * 2**20),
        )(mode_shapes.reshape(2, rows, width), mass_blocks, block_cols, send_lists)

    return jax.shard_map(
        local,
        mesh=mesh,
        in_specs=(
            P("sweep", None, "dof", None),
            P(None, None, None, "dof"),
            P(None, "dof"),
            P("dof", None, None),
        ),
        out_specs=P("dof", "sweep", None),
        check_vma=False,
    )
```

time: 112 us -> 95.4 us (0.85)
  the two profiles are of different devices: /device:TPU:102 before, /device:TPU:64 now
where the time goes in v2:
time: 95.4 us; the launch traced here: 95.1 us
  Pallas kernels  91 us (95%)
  local copies, waits for them, and re-layouts  4.09 us (4%)
    pallas_call x1, Pallas kernels, local(): pl.pallas_call(lambda *refs: margins_kernel(n_sweep, n_dof, *refs), out_s...  91 us
    unnamed x9, local copies, waits for them, and re-layouts  4.09 us

profile of v2, /device:TPU:64, one launch (start us, length us, event | category | flops | bytes accessed | tf_op | source)
XLA Modules:
  0.0 95.1 jit_solution(16277115309501150817)
XLA Ops:
  0.0 0.0 copy-start.3
  0.0 0.7 copy-done.3
  0.7 0.0 copy-start
  0.7 1.2 %copy-done = bf16[2,3,320,256]{3,2,1,0:T(8,128)(2,1)S(1)} copy-done((bf16[2,3,320,256]{3,2,1,0:T(8,128)(2,1)S(1)}, bf16[2,3,320,256]{3,2,1,0:T(8,128)(2,1)}, u32[]{:S(2)}) %copy-start) | copy-done | bytes 983064
  1.9 0.0 copy-start.1
  1.9 0.9 copy-done.1
  2.8 0.0 copy-start.2
  2.8 0.7 copy-done.2
  3.5 91.0 %shard_map.46 = f32[8,2,256]{2,1,0:T(2,128)S(1)} custom-call(bf16[2,960,256]{2,1,0:T(8,128)(2,1)S(1)} %bitcast.1, f32[3,3,8,320]{3,2,1,0:T(8,128)S(1)} %copy-done.1, s32[8,320]{1,0:T(8,128)S(1)} %copy-done.2, s32[1,2,128]{2,1,0:T(2,128)S(1)} %copy-done.3), custom_call_target="tpu_custom_call" | custom-call | tf_op jit(solution)/shard_map/pallas_call | solution.py:285
  94.5 0.6 copy.6
Async XLA Ops:
  0.0 0.7 copy-start.3
  0.7 1.2 %copy-start = (bf16[2,3,320,256]{3,2,1,0:T(8,128)(2,1)S(1)}, bf16[2,3,320,256]{3,2,1,0:T(8,128)(2,1)}, u32[]{:S(2)}) copy-start(bf16[2,3,320,256]{3,2,1,0:T(8,128)(2,1)} %param.4) | copy-start | bytes 2949124
  1.9 0.9 copy-start.1
  2.8 0.7 copy-start.2

commit v3 on v2

--- a/solution.py
+++ b/solution.py
@@ -10,10 +10,11 @@
 HALVES = 2
 GROUP = 2
 PARTS = 6
+FIRST = 1
 WINDOW = 4
+CUT = 4
 C_PARTS = 6
-C_FROM = 0
-CUT = 8
+E_SOON = 1
 PACK = 1024
 LISTS = 384
 
@@ -26,9 +27,9 @@
     return lax.dot_general(a, b, (((0,), (0,)), ((), ())), preferred_element_type=F32)
 
 
-def margins_kernel(n_sweep, n_dof, modes_in, mass_in, cols_in, lists_in, out, modes, mass, cols, lists, fq, fr, cb, mass_own, cols_own, pk_own, pk_q, pk_r, cols_q, cols_r,
+def margins_kernel(n_sweep, n_dof, modes_in, mass_in, cols_in, lists_in, out, modes, mass, cols, lists, fq, fr, cb, relay, mass_own, cols_own, pk_own, pk_q, pk_r, cols_q, cols_r,
                    mt_hi, mt_lo, mq_hi, mq_lo, mr_hi, mr_lo, ya_own, ya_halo, yb, g_q, g_r, cs_q, cs_r, part, acc_bt, rsb, tot,
-                   last, z_ss, z_rs, x_ss, x_rs, c_ss, c_rs, m_ss, m_rs, e_ss, e_rs, a_ss, a_rs, b_ss, b_rs, in_s):
+                   last, z_ss, z_rs, x_ss, x_rs, c_ss, c_rs, ri_ss, ri_rs, ro_ss, m_ss, m_rs, e_ss, e_rs, a_ss, a_rs, b_ss, b_rs, in_s):
     nodes, halo, width = cols.shape[1], lists.shape[2], modes.shape[2]
     rows = 3 * nodes
     planes = n_dof // 2
@@ -50,16 +51,83 @@
     is_last = w == n_sweep - 1
 
     barrier = pltpu.get_barrier_semaphore()
-    greeted = [far, sweep_step(1), sweep_step(-1)]
+    greeted = [far]
     greeted += [groupmate(t) for t in range(1, GROUP)]
     greeted += [plane(k + t) for t in range(1, planes)]
     for device in greeted:
         pl.semaphore_signal(barrier, inc=1, device_id=device, device_id_type=MESH)
 
+    @pl.when(w > 0)
+    def _():
+        pl.semaphore_signal(barrier, inc=1, device_id=sweep_step(-1), device_id_type=MESH)
+
+    @pl.when(w > 1)
+    def _():
+        pl.semaphore_signal(barrier, inc=1, device_id=sweep_step(-2), device_id_type=MESH)
+
+    @pl.when(jnp.logical_not(is_last))
+    def _():
+        pl.semaphore_signal(barrier, inc=1, device_id=sweep_step(1), device_id_type=MESH)
+
+    @pl.when(w < n_sweep - 2)
+    def _():
+        pl.semaphore_signal(barrier, inc=1, device_id=sweep_step(2), device_id_type=MESH)
+
     loads = [pltpu.make_async_copy(src, dst, in_s.at[i])
              for i, (src, dst) in enumerate(((mass_in, mass), (cols_in, cols), (lists_in, lists), (modes_in, modes)))]
     for load in loads:
         load.start()
+    beside = [w > 0, w > 1, w < n_sweep - 1, w < n_sweep - 2]
+    pl.semaphore_wait(barrier, len(greeted) + sum(jnp.where(near, 1, 0) for near in beside))
+
+    def remote(src, dst, send, recv, device):
+        return pltpu.make_async_remote_copy(src_ref=src, dst_ref=dst, send_sem=send, recv_sem=recv, device_id=device,
+                                            device_id_type=MESH)
+
+    chunks = [(c, h) for h in range(HALVES) for c in range(PARTS)]
+
+    def piece(ref, c, h):
+        return ref.at[pl.ds(c * (rows // PARTS), rows // PARTS), pl.ds(h * half, half)]
+
+    def strip(ref, c):
+        return ref.at[pl.ds(c * (rows // C_PARTS), rows // C_PARTS)]
+
+    x_next = plane(k + 1 - 2 * z_hi)
+    mine = pl.ds(pl.multiple_of(seat * (PACK // GROUP), PACK // GROUP), PACK // GROUP)
+    z_copies = [remote(piece(modes_in.at[1], c, h), piece(fq, c, h), z_ss.at[i], z_rs.at[i], far) for i, (c, h) in enumerate(chunks)]
+    x_copies = [remote(piece(fq, c, h), piece(fr, c, h), x_ss.at[i], x_rs.at[i], x_next) for i, (c, h) in enumerate(chunks)]
+    c_copies = [remote(strip(modes_in.at[0], i), strip(cb, i), c_ss.at[i], c_rs.at[i], sweep_step(-1)) for i in range(C_PARTS)]
+    c_split = C_PARTS // 2
+    in_copies = [remote(strip(modes_in.at[0], i), strip(relay, i - c_split), ri_ss.at[i - c_split], ri_rs.at[i - c_split], sweep_step(1))
+                 for i in range(c_split, C_PARTS)]
+    out_copies = [remote(strip(relay, i - c_split), strip(cb, i), ro_ss.at[i - c_split], c_rs.at[i], sweep_step(-2))
+                  for i in range(c_split, C_PARTS)]
+    core = lax.rem(w, 2)
+    own_copy = remote(pk_own.at[:, :, mine], pk_q.at[:, :, mine], m_ss.at[1], m_rs.at[1], far)
+    e_copies = [remote(pk_q.at[:, :, mine], pk_q.at[:, :, mine], e_ss.at[t - 1], e_rs.at[t - 1], groupmate(t)) for t in range(1, GROUP)]
+    pack_copy = remote(pk_q, pk_r, m_ss.at[2], m_rs.at[2], x_next)
+
+    pumped = [0]
+
+    def pump(twelfths):
+        upto = len(chunks) * twelfths // 12
+        for i in range(pumped[0], upto):
+            z_copies[i].wait_recv()
+            x_copies[i].start()
+            if i + WINDOW < len(chunks):
+                @pl.when(w // 2 >= CUT)
+                def _():
+                    z_copies[i + WINDOW].start()
+        pumped[0] = upto
+
+    @pl.when(jnp.logical_and(core == 0, w > 0))
+    def _():
+        for copy in in_copies:
+            copy.start()
+
+    for i in range(FIRST):
+        z_copies[i].start()
+
     for load in loads[0:3]:
         load.wait()
 
@@ -78,45 +146,24 @@
     pk_own[1, 0:1, :] = wide([columns[b:b + 1] for b in (4, 5, 6)])
     pk_own[2, 0:1, :] = wide([columns[7:8], jnp.zeros((1, LISTS - nodes), F32), own_lists[0:1], own_lists[1:2]])
 
-    pl.semaphore_wait(barrier, len(greeted))
-
-    def remote(src, dst, send, recv, device):
-        return pltpu.make_async_remote_copy(src_ref=src, dst_ref=dst, send_sem=send, recv_sem=recv, device_id=device,
-                                            device_id_type=MESH)
-
-    chunks = [(c, h) for h in range(HALVES) for c in range(PARTS)]
-
-    def piece(ref, c, h):
-        return ref.at[pl.ds(c * (rows // PARTS), rows // PARTS), pl.ds(h * half, half)]
-
-    def strip(ref, c):
-        return ref.at[pl.ds(c * (rows // C_PARTS), rows // C_PARTS)]
-
-    x_next = plane(k + 1 - 2 * z_hi)
-    mine = pl.ds(pl.multiple_of(seat * (PACK // GROUP), PACK // GROUP), PACK // GROUP)
-    z_copies = [remote(piece(modes_in.at[1], c, h), piece(fq, c, h), z_ss.at[i], z_rs.at[i], far) for i, (c, h) in enumerate(chunks)]
-    x_copies = [remote(piece(fq, c, h), piece(fr, c, h), x_ss.at[i], x_rs.at[i], x_next) for i, (c, h) in enumerate(chunks)]
-    c_copies = [remote(strip(modes_in.at[0], i), strip(cb, i), c_ss.at[i], c_rs.at[i], sweep_step(-1)) for i in range(C_PARTS)]
-    own_copy = remote(pk_own.at[:, :, mine], pk_q.at[:, :, mine], m_ss.at[1], m_rs.at[1], far)
-    e_copies = [remote(pk_q.at[:, :, mine], pk_q.at[:, :, mine], e_ss.at[t - 1], e_rs.at[t - 1], groupmate(t)) for t in range(1, GROUP)]
-    pack_copy = remote(pk_q, pk_r, m_ss.at[2], m_rs.at[2], x_next)
-
-    def pump(i):
-        z_copies[i].wait_recv()
-        x_copies[i].start()
-        if i + WINDOW < len(chunks):
-            z_copies[i + WINDOW].start()
-        if C_FROM <= i < C_FROM + C_PARTS:
-            @pl.when(w > 0)
-            def _():
-                c_copies[i - C_FROM].start()
-
     own_copy.start()
+    for i in range(FIRST, WINDOW):
+        z_copies[i].start()
+
+    @pl.when(w > 0)
+    def _():
+        for copy in c_copies[:c_split]:
+            copy.start()
+
+    @pl.when(core == 1)
+    def _():
+        for copy in c_copies[c_split:]:
+            copy.start()
 
     @pl.when(w // 2 < CUT)
     def _():
-        for i in range(WINDOW):
-            z_copies[i].start()
+        for copy in z_copies[WINDOW:]:
+            copy.start()
 
     def build(masses, columns, slots, offset, begin, count, hi, lo):
         def body(g, carry):
@@ -169,33 +216,35 @@
     own_copy.wait_recv()
     for copy in e_copies:
         copy.start()
+
+    @pl.when(jnp.logical_and(core == 1, w > 1))
+    def _():
+        for arrived, copy in zip(in_copies, out_copies):
+            arrived.wait_recv()
+            copy.start()
+
     build(mass_own, cols_own, range(8), 0, ext // 2, ext, mt_hi, mt_lo)
-
-    @pl.when(w // 2 >= CUT)
-    def _():
-        for i in range(WINDOW):
-            z_copies[i].start()
-
-    for copy in e_copies:
-        copy.wait_recv()
-    pack_copy.start()
     loads[3].wait()
-
     for d in range(3):
-        pump(d)
         first = dot(mt_hi[d], modes[0]) + dot(mt_lo[d], modes[0])
         ya_own[pl.ds(d * nodes, nodes), :] = first[0:nodes].astype(BF16)
         ya_halo[d] = first[nodes:].astype(BF16)
-    pump(3)
+        pump(d + 1)
+    for copy in e_copies[:E_SOON * len(e_copies)]:
+        copy.wait_recv()
+    if E_SOON:
+        pack_copy.start()
     part[0] = dot_t(ya_own[...], modes[1])
+    pump(4)
     for d in range(3):
         second = dot(mt_hi[d, 0:nodes], modes[1]) + dot(mt_lo[d, 0:nodes], modes[1])
         yb[pl.ds(d * nodes, nodes), :] = second.astype(BF16)
-    pump(4)
+    pump(5)
+    if not E_SOON:
+        for copy in e_copies:
+            copy.wait_recv()
+        pack_copy.start()
     side_rows(pk_q, cols_q, 1 - z_hi, 1 - z_hi, z_hi, mq_hi, mq_lo, g_q)
-    pump(5)
-    pack_copy.wait_recv()
-    side_rows(pk_r, cols_r, z_hi, z_hi, 1 - z_hi, mr_hi, mr_lo, g_r)
     pump(6)
     use_first(fq, g_q, 0)
     pump(7)
@@ -212,8 +261,11 @@
     acc_bt[...] = dot_t(cb[...], yb[...])
     side_partner(z_hi, cs_q)
     side_partner(1 - z_hi, cs_r)
+    pump(8)
     use_second(fq, mq_hi, mq_lo, cs_q, 0)
-    pump(8)
+    pack_copy.wait_recv()
+    side_rows(pk_r, cols_r, z_hi, z_hi, 1 - z_hi, mr_hi, mr_lo, g_r)
+    pump(9)
 
     share = width // n_dof
     pair = 2 * share
@@ -230,8 +282,7 @@
     for h in range(HALVES):
         lanes = slice(h * half, (h + 1) * half)
         if h > 0:
-            for i in range(9, h * PARTS + PARTS):
-                pump(i)
+            pump(12)
             use_first(fq, g_q, h)
             use_second(fq, mq_hi, mq_lo, cs_q, h)
         for i in range(h * PARTS, h * PARTS + PARTS):
@@ -262,7 +313,22 @@
 
     @pl.when(w > 0)
     def _():
-        for copy in c_copies:
+        for copy in c_copies[:c_split]:
+            copy.wait_send()
+
+    @pl.when(core == 1)
+    def _():
+        for copy in c_copies[c_split:]:
+            copy.wait_send()
+
+    @pl.when(jnp.logical_and(core == 1, w > 1))
+    def _():
+        for copy in out_copies:
+            copy.wait_send()
+
+    @pl.when(jnp.logical_and(core == 0, w > 0))
+    def _():
+        for copy in in_copies:
             copy.wait_send()
 
     own_copy.wait_send()
@@ -290,6 +356,7 @@
             scratch_shapes=[
                 vmem((2, rows, width), BF16), vmem(mass_blocks.shape, F32), vmem(block_cols.shape, jnp.int32), vmem(send_lists.shape, jnp.int32),
                 vmem((rows, width), BF16), vmem((rows, width), BF16), vmem((rows, width), BF16),
+                vmem((rows // 2, width), BF16),
                 vmem((3, 8, rows), F32), vmem((8, rows), F32),
                 vmem((3, 8, PACK), F32), vmem((3, 8, PACK), F32), vmem((3, 8, PACK), F32), vmem((8, rows), F32), vmem((8, rows), F32),
                 vmem((3, ext, rows), BF16), vmem((3, ext, rows), BF16),
@@ -302,7 +369,7 @@
                 vmem((planes - 1, 2, 2 * share, width), F32),
                 vmem((2, 2, share, width), F32), vmem((2, share, width), F32),
                 dma((HALVES * PARTS,)), dma((HALVES * PARTS,)), dma((HALVES * PARTS,)), dma((HALVES * PARTS,)),
-                dma((C_PARTS,)), dma((C_PARTS,)), dma((4,)), dma((4,)), dma((GROUP - 1,)), dma((GROUP - 1,)),
+                dma((C_PARTS,)), dma((C_PARTS,)), dma((C_PARTS // 2,)), dma((C_PARTS // 2,)), dma((C_PARTS // 2,)), dma((4,)), dma((4,)), dma((GROUP - 1,)), dma((GROUP - 1,)),
                 dma((HALVES, planes - 1)), dma((HALVES, planes - 1)), dma((planes - 1,)), dma((planes - 1,)), dma((4,)),
             ],
             compiler_params=pltpu.CompilerParams(collective_id=0, has_side_effects=True, vmem_limit_bytes=40 * 2**20),

time: 95.4 us -> 93.9 us (0.984)
  the two profiles are of different devices: /device:TPU:64 before, /device:TPU:160 now
where the time goes in v3:
time: 93.9 us; the launch traced here: 93.7 us
  Pallas kernels  89.6 us (95%)
  local copies, waits for them, and re-layouts  4.09 us (4%)
    pallas_call x1, Pallas kernels, local(): pl.pallas_call(lambda *refs: margins_kernel(n_sweep, n_dof, *refs), out_s...  89.6 us
    unnamed x9, local copies, waits for them, and re-layouts  4.09 us

profile of v3, /device:TPU:160, one launch (start us, length us, event | category | flops | bytes accessed | tf_op | source)
XLA Modules:
  0.0 93.7 jit_solution(7190275761585777603)
XLA Ops:
  0.0 0.0 copy-start.3
  0.0 0.7 copy-done.3
  0.7 0.0 copy-start
  0.7 1.2 %copy-done = bf16[2,3,320,256]{3,2,1,0:T(8,128)(2,1)S(1)} copy-done((bf16[2,3,320,256]{3,2,1,0:T(8,128)(2,1)S(1)}, bf16[2,3,320,256]{3,2,1,0:T(8,128)(2,1)}, u32[]{:S(2)}) %copy-start) | copy-done | bytes 983064
  1.9 0.0 copy-start.1
  1.9 0.9 copy-done.1
  2.8 0.0 copy-start.2
  2.8 0.7 copy-done.2
  3.5 89.6 %shard_map.46 = f32[8,2,256]{2,1,0:T(2,128)S(1)} custom-call(bf16[2,960,256]{2,1,0:T(8,128)(2,1)S(1)} %bitcast.1, f32[3,3,8,320]{3,2,1,0:T(8,128)S(1)} %copy-done.1, s32[8,320]{1,0:T(8,128)S(1)} %copy-done.2, s32[1,2,128]{2,1,0:T(2,128)S(1)} %copy-done.3), custom_call_target="tpu_custom_call" | custom-call | tf_op jit(solution)/shard_map/pallas_call | solution.py:351
  93.1 0.6 copy.6
Async XLA Ops:
  0.0 0.7 copy-start.3
  0.7 1.2 %copy-start = (bf16[2,3,320,256]{3,2,1,0:T(8,128)(2,1)S(1)}, bf16[2,3,320,256]{3,2,1,0:T(8,128)(2,1)}, u32[]{:S(2)}) copy-start(bf16[2,3,320,256]{3,2,1,0:T(8,128)(2,1)} %param.4) | copy-start | bytes 2949124
  1.9 0.9 copy-start.1
  2.8 0.7 copy-start.2

commit v4 on v3

--- a/solution.py
+++ b/solution.py
@@ -12,6 +12,7 @@
 PARTS = 6
 FIRST = 1
 WINDOW = 4
+DEPTH = 768
 CUT = 4
 C_PARTS = 6
 E_SOON = 1
@@ -193,23 +194,25 @@
             columns[b:b + 1, :] = jnp.concatenate([pk[(b - 1) // 3, 0:1, at:at + nodes]] * 3, axis=1)
         there = one_hot(jnp.where(row_there == 0, pk[2, 0:1, LISTS:LISTS + halo], pk[2, 0:1, LISTS + halo:LISTS + 2 * halo]))
         build(pk, columns, range(1, 8), nodes + halo * seg_there, 0, halo, hi, lo)
-        spread = [dot(there, ya_halo[d, pl.ds(pl.multiple_of(halo * seg_here, halo), halo), :]).T for d in range(3)]
-        g[...] = jnp.concatenate(spread, axis=1).astype(BF16)
+        fanned = [dot(there, ya_halo[d, pl.ds(pl.multiple_of(halo * seg_here, halo), halo), :]).T for d in range(3)]
+        g[...] = jnp.concatenate(fanned, axis=1).astype(BF16)
 
     def side_partner(row_here, cs):
         here = one_hot(jnp.where(row_here == 0, lists[0, 0:1, :], lists[0, 1:2, :]).astype(F32))
         for d in range(3):
             cs[:, d * halo:(d + 1) * halo] = dot_t(cb[pl.ds(d * nodes, nodes), :], here).astype(BF16)
 
-    def use_first(field, g, h):
+    def use_first(field, g, h, begin, end):
         lanes = slice(h * half, (h + 1) * half)
-        part[0, :, lanes] += dot(g[...], field[:, lanes])
-
-    def use_second(field, hi, lo, cs, h):
-        lanes = slice(h * half, (h + 1) * half)
-        block = field[:, lanes]
-        y = (dot(hi[...].reshape(3 * halo, rows), block) + dot(lo[...].reshape(3 * halo, rows), block)).astype(BF16)
-        acc_bt[:, lanes] += dot(cs[...], y)
+        part[0, :, lanes] += dot(g[:, begin:end], field[begin:end, lanes])
+
+    def spread(field, hi, lo, h, begin, end):
+        block = field[begin:end, h * half:(h + 1) * half]
+        both = [ref[:, :, begin:end].reshape(3 * halo, end - begin) for ref in (hi, lo)]
+        return dot(both[0], block) + dot(both[1], block)
+
+    def use_second(y, cs, h):
+        acc_bt[:, h * half:(h + 1) * half] += dot(cs[...], y.astype(BF16))
 
     ext = nodes + 2 * halo
     build(mass_own, cols_own, range(8), 0, 0, ext // 2, mt_hi, mt_lo)
@@ -246,7 +249,7 @@
         pack_copy.start()
     side_rows(pk_q, cols_q, 1 - z_hi, 1 - z_hi, z_hi, mq_hi, mq_lo, g_q)
     pump(6)
-    use_first(fq, g_q, 0)
+    use_first(fq, g_q, 0, 0, rows)
     pump(7)
 
     @pl.when(jnp.logical_not(is_last))
@@ -262,7 +265,7 @@
     side_partner(z_hi, cs_q)
     side_partner(1 - z_hi, cs_r)
     pump(8)
-    use_second(fq, mq_hi, mq_lo, cs_q, 0)
+    use_second(spread(fq, mq_hi, mq_lo, 0, 0, rows), cs_q, 0)
     pack_copy.wait_recv()
     side_rows(pk_r, cols_r, z_hi, z_hi, 1 - z_hi, mr_hi, mr_lo, g_r)
     pump(9)
@@ -283,14 +286,21 @@
         lanes = slice(h * half, (h + 1) * half)
         if h > 0:
             pump(12)
-            use_first(fq, g_q, h)
-            use_second(fq, mq_hi, mq_lo, cs_q, h)
-        for i in range(h * PARTS, h * PARTS + PARTS):
-            x_copies[i].wait_recv()
-        use_first(fr, g_r, h)
+            use_first(fq, g_q, h, 0, rows)
+            use_second(spread(fq, mq_hi, mq_lo, h, 0, rows), cs_q, h)
+        *ahead, final = x_copies[h * PARTS:h * PARTS + PARTS]
+        for copy in ahead:
+            copy.wait_recv()
+        use_first(fr, g_r, h, 0, DEPTH)
+        y = spread(fr, mr_hi, mr_lo, h, 0, DEPTH)
+        if h > 0:
+            for copy in a_copies[:planes - 1]:
+                copy.wait_recv()
+        final.wait_recv()
+        use_first(fr, g_r, h, DEPTH, rows)
         for t in range(1, planes):
             a_copies[h * (planes - 1) + t - 1].start()
-        use_second(fr, mr_hi, mr_lo, cs_r, h)
+        use_second(y + spread(fr, mr_hi, mr_lo, h, DEPTH, rows), cs_r, h)
         part[1, lanes, :] = acc_bt[:, lanes].T
         for t in range(1, planes):
             @pl.when(lax.rem(k + t, planes) // (planes // HALVES) == h)
@@ -299,8 +309,7 @@
 
     total = part[:, pl.ds(pl.multiple_of(k * pair, pair), pair), :]
     for t in range(1, planes):
-        for h in range(HALVES):
-            a_copies[h * (planes - 1) + t - 1].wait_recv()
+        a_copies[planes - 1 + t - 1].wait_recv()
         b_copies[t - 1].wait_recv()
         total = total + rsb[t - 1]
     tot[:, 0] = total[:, 0:share]

time: 93.9 us -> 93.8 us (level)
  no operation moved by 1% of the time
where the time goes in v4:
time: 93.8 us; the launch traced here: 93.6 us
  Pallas kernels  89.5 us (95%)
  local copies, waits for them, and re-layouts  4.09 us (4%)
    pallas_call x1, Pallas kernels, local(): pl.pallas_call(lambda *refs: margins_kernel(n_sweep, n_dof, *refs), out_s...  89.5 us
    unnamed x9, local copies, waits for them, and re-layouts  4.09 us

profile of v4, /device:TPU:160, one launch (start us, length us, event | category | flops | bytes accessed | tf_op | source)
XLA Modules:
  0.0 93.6 jit_solution(2742556766377982485)
XLA Ops:
  0.0 0.0 copy-start.3
  0.0 0.7 copy-done.3
  0.7 0.0 copy-start
  0.7 1.2 %copy-done = bf16[2,3,320,256]{3,2,1,0:T(8,128)(2,1)S(1)} copy-done((bf16[2,3,320,256]{3,2,1,0:T(8,128)(2,1)S(1)}, bf16[2,3,320,256]{3,2,1,0:T(8,128)(2,1)}, u32[]{:S(2)}) %copy-start) | copy-done | bytes 983064
  1.9 0.0 copy-start.1
  1.9 0.9 copy-done.1
  2.8 0.0 copy-start.2
  2.8 0.7 copy-done.2
  3.5 89.5 %shard_map.46 = f32[8,2,256]{2,1,0:T(2,128)S(1)} custom-call(bf16[2,960,256]{2,1,0:T(8,128)(2,1)S(1)} %bitcast.1, f32[3,3,8,320]{3,2,1,0:T(8,128)S(1)} %copy-done.1, s32[8,320]{1,0:T(8,128)S(1)} %copy-done.2, s32[1,2,128]{2,1,0:T(2,128)S(1)} %copy-done.3), custom_call_target="tpu_custom_call" | custom-call | tf_op jit(solution)/shard_map/pallas_call | solution.py:360
  93.0 0.6 copy.6
Async XLA Ops:
  0.0 0.7 copy-start.3
  0.7 1.2 %copy-start = (bf16[2,3,320,256]{3,2,1,0:T(8,128)(2,1)S(1)}, bf16[2,3,320,256]{3,2,1,0:T(8,128)(2,1)}, u32[]{:S(2)}) copy-start(bf16[2,3,320,256]{3,2,1,0:T(8,128)(2,1)} %param.4) | copy-start | bytes 2949124
  1.9 0.9 copy-start.1
  2.8 0.7 copy-start.2
